TPU v7x, 32 devices: a whole 2x2x4 slice. The times are simulated.
32 devices in a mesh: dom: 32 (over z, y, x, core).
Axes of the slice: x: 2, y: 2, z: 4, core: 2. Of those that a mesh axis runs over, the one named last changes fastest.
Arguments:
- features: float32 [131072, 100], P('dom'), may hold values from -6 to 6
- labels: int32 [131072], P('dom'), may hold values from 0 to 46
- train_mask: int32 [131072], P('dom'), may hold values from 0 to 1, as said below
- boundary: int32 [3, 4096], P(None, 'dom'), may hold values from 0 to 4095
- neighbours: int32 [3, 131072, 16], P(None, 'dom'), may hold values from 0 to 8191, as said below
- counts: int32 [3, 131072], P(None, 'dom'), may hold values from 1 to 16, as said below
- first_weight: float32 [200, 256], P(None, 'dom'), may hold values from -0.4375 to 0.4375
- rest_weight: float32 [2, 512, 256], P(None, None, 'dom'), may hold values from -0.25 to 0.25
- head_weight: float32 [256, 47], P('dom'), may hold values from -0.375 to 0.375
- norm_params: float32 [3, 2, 256], replicated
- head_bias: float32 [47], replicated, may hold values from -3 to 3
- first_row: float32 [200], replicated, may hold values from 6.1035155e-09 to 2.4414062e-08
- first_col: float32 [256], P('dom'), may hold values from 6.1035155e-09 to 2.4414062e-08
- rest_row: float32 [2, 512], replicated, may hold values from 5.340576e-09 to 2.1362304e-08
- rest_col: float32 [2, 256], P(None, 'dom'), may hold values from 5.340576e-09 to 2.1362304e-08
- head_row: float32 [256], P('dom'), may hold values from 1.14440915e-07 to 4.5776366e-07
- head_col: float32 [47], replicated, may hold values from 1.14440915e-07 to 4.5776366e-07
- norm_state: float32 [3, 2, 256], replicated, may hold values from 7.629395e-09 to 6.103516e-08
- bias_state: float32 [47], replicated, may hold values from 3.0517577e-07 to 1.2207031e-06
Outputs:
- loss_sum: float32 [], replicated
- label_count: float32 [], replicated
- first_new: float32 [200, 256], P(None, 'dom')
- rest_new: float32 [2, 512, 256], P(None, None, 'dom')
- head_new: float32 [256, 47], P('dom')
- norm_new: float32 [3, 2, 256], replicated
- bias_new: float32 [47], replicated
- first_grad: float32 [200, 256], P(None, 'dom')
- rest_grad: float32 [2, 512, 256], P(None, None, 'dom')
- head_grad: float32 [256, 47], P('dom')
- norm_grad: float32 [3, 2, 256], replicated
- bias_grad: float32 [47], replicated
- first_row_new: float32 [200], replicated
- first_col_new: float32 [256], P('dom')
- rest_row_new: float32 [2, 512], replicated
- rest_col_new: float32 [2, 256], P(None, 'dom')
- head_row_new: float32 [256], P('dom')
- head_col_new: float32 [47], replicated
- norm_state_new: float32 [3, 2, 256], replicated
- bias_state_new: float32 [47], replicated
- first_copy: bfloat16 [200, 256], P(None, 'dom')
- rest_copy: bfloat16 [2, 512, 256], P(None, None, 'dom')
- head_copy: bfloat16 [256, 47], P('dom')
- norm_copy: bfloat16 [3, 2, 256], replicated
Inputs may be any that keep to these rules, and one draw needn't show every extreme that they name: `neighbours`: entries at slots k >= counts are 0. A value t + 4096 names boundary slot t; the slots that partition q publishes are used only below a kept number that runs from 42 to 128 over the partitions, both ends reached; the last partition keeps all 128. In each layer, node 0's slot 0 names the last boundary slot. `counts`: each layer's first node has 16 kept neighbours. `train_mask`: node 0 is labelled.
All inputs are finite; a program needn't handle non-finite values.
Results may differ from a plain program's by a relative error of at most 0.012.
The roundings to bfloat16 on the way count: a program that leaves them out, or rounds other values in their place, can miss the bound.
Values may be sent and summed in bfloat16 or wider, within the bound.
No kernel may reach another device: no remote copies, remote signals or barrier semaphores. Data moves between devices by JAX's collectives and lax.ppermute only.
A program may use at most 256 MiB of HBM per device.

v0:
```python
import jax
import jax.numpy as jnp
from jax import lax
from jax.sharding import PartitionSpec as P

LEARN_RATE = 0.03
VECTOR_RATE = 0.25
SQUARE_EPS = 1e-30


def slot_use(kept_count, slot_total):
    return jnp.arange(slot_total, dtype=jnp.int32)[None, :] < kept_count[:, None]


def aggregate(rounded, shared_rows, slot_ids, kept_count):
    source = jnp.concatenate([rounded, shared_rows], axis=0)
    picked = source[slot_ids]
    slot_live = slot_use(kept_count, slot_ids.shape[1]).astype(jnp.bfloat16)
    summed = jnp.einsum("nkf,nk->nf", picked, slot_live, preferred_element_type=jnp.float32)
    return (summed / kept_count[:, None].astype(jnp.float32)).astype(jnp.bfloat16)


def layer_norm(pre_norm):
    centre = pre_norm - jnp.mean(pre_norm, axis=1, keepdims=True)
    inv_spread = lax.rsqrt(jnp.mean(centre * centre, axis=1, keepdims=True) + 1e-05)
    return (centre * inv_spread, inv_spread)


def layer_forward(hidden, weight, norm_pair, boundary_rows, slot_ids, kept_count):
    rounded = hidden.astype(jnp.bfloat16)
    shared_rows = lax.all_gather(rounded[boundary_rows], "dom", axis=0, tiled=True)
    mean_in = aggregate(rounded, shared_rows, slot_ids, kept_count)
    pre_norm = jnp.dot(
        jnp.concatenate([rounded, mean_in], axis=1), weight, preferred_element_type=jnp.float32
    )
    normed, inv_spread = layer_norm(pre_norm)
    return (jax.nn.silu(normed * norm_pair[0] + norm_pair[1]), rounded, mean_in, pre_norm)


def layer_backward(
    d_hidden,
    weight,
    norm_pair,
    rounded,
    mean_in,
    pre_norm,
    boundary_rows,
    slot_ids,
    kept_count,
    need_input,
):
    normed, inv_spread = layer_norm(pre_norm)
    normed_out = normed * norm_pair[0] + norm_pair[1]
    sig_out = jax.nn.sigmoid(normed_out)
    d_out = d_hidden * sig_out * (1.0 + normed_out * (1.0 - sig_out))
    d_pair = jnp.stack([jnp.sum(d_out * normed, axis=0), jnp.sum(d_out, axis=0)])
    d_normed = d_out * norm_pair[0]
    d_pre = inv_spread * (
        d_normed
        - jnp.mean(d_normed, axis=1, keepdims=True)
        - normed * jnp.mean(d_normed * normed, axis=1, keepdims=True)
    )
    d_pre = d_pre.astype(jnp.bfloat16)
    joined = jnp.concatenate([rounded, mean_in], axis=1)
    d_weight = jnp.einsum("nf,ng->fg", joined, d_pre, preferred_element_type=jnp.float32)
    if not need_input:
        return (None, d_weight, d_pair)
    d_joined = jnp.einsum("ng,fg->nf", d_pre, weight, preferred_element_type=jnp.float32)
    feat_width = rounded.shape[1]
    node_rows = rounded.shape[0]
    part_total = lax.axis_size("dom")
    own_slots = boundary_rows.shape[0]
    shared_total = own_slots * part_total
    per_slot = d_joined[:, feat_width:] / kept_count[:, None].astype(jnp.float32)
    slot_live = slot_use(kept_count, slot_ids.shape[1]).astype(jnp.float32)
    spread_out = per_slot[:, None, :] * slot_live[:, :, None]
    d_source = jnp.zeros((node_rows + shared_total, feat_width), jnp.float32)
    d_source = d_source.at[slot_ids.reshape(-1)].add(spread_out.reshape(-1, feat_width))
    d_shared = lax.psum_scatter(d_source[node_rows:], "dom", scatter_dimension=0, tiled=True)
    d_input = d_joined[:, :feat_width] + d_source[:node_rows]
    d_input = d_input.at[boundary_rows].add(d_shared)
    return (d_input, d_weight, d_pair)


def factored_step(weight, gradient, row_new, col_new, row_mean):
    estimate = row_new[..., :, None] * col_new[..., None, :] / row_mean[..., None, None]
    return weight - LEARN_RATE * gradient * lax.rsqrt(estimate)


def vector_step(param, gradient, state):
    state_new = 0.5 * state + 0.5 * (gradient * gradient + SQUARE_EPS)
    return (param - VECTOR_RATE * gradient * lax.rsqrt(state_new), state_new)


def on_device(
    features,
    labels,
    train_mask,
    boundary,
    neighbours,
    counts,
    first_weight,
    rest_weight,
    head_weight,
    norm_params,
    head_bias,
    first_row,
    first_col,
    rest_row,
    rest_col,
    head_row,
    head_col,
    norm_state,
    bias_state,
):
    full_first, full_rest, full_head = (
        lax.all_gather(first_weight.astype(jnp.bfloat16), "dom", axis=1, tiled=True),
        lax.all_gather(rest_weight.astype(jnp.bfloat16), "dom", axis=2, tiled=True),
        lax.all_gather(head_weight.astype(jnp.bfloat16), "dom", axis=0, tiled=True),
    )
    depth = rest_weight.shape[0] + 1
    weights = [full_first] + [full_rest[layer_id] for layer_id in range(depth - 1)]
    hidden = features
    saved = []
    for layer_id in range(depth):
        hidden, rounded, mean_in, pre_norm = layer_forward(
            hidden,
            weights[layer_id],
            norm_params[layer_id],
            boundary[layer_id],
            neighbours[layer_id],
            counts[layer_id],
        )
        saved.append((rounded, mean_in, pre_norm))
    top_rows = hidden.astype(jnp.bfloat16)
    logits = jnp.dot(top_rows, full_head, preferred_element_type=jnp.float32) + head_bias
    peak = jnp.max(logits, axis=1, keepdims=True)
    log_total = peak[:, 0] + jnp.log(jnp.sum(jnp.exp(logits - peak), axis=1))
    target_hot = labels[:, None] == jnp.arange(full_head.shape[1], dtype=jnp.int32)[None, :]
    picked = jnp.sum(jnp.where(target_hot, logits, 0.0), axis=1)
    label_live = train_mask.astype(jnp.float32)
    loss_sum, label_count = lax.psum(
        (jnp.sum(label_live * (log_total - picked)), jnp.sum(label_live)), "dom"
    )
    probs = jnp.exp(logits - log_total[:, None])
    d_logits = (
        (probs - target_hot.astype(jnp.float32)) * label_live[:, None] / label_count
    ).astype(jnp.bfloat16)
    d_head = jnp.einsum("nf,nc->fc", top_rows, d_logits, preferred_element_type=jnp.float32)
    d_bias = jnp.sum(d_logits.astype(jnp.float32), axis=0)
    d_hidden = jnp.einsum("nc,fc->nf", d_logits, full_head, preferred_element_type=jnp.float32)
    d_weights = [None] * depth
    d_pairs = [None] * depth
    for layer_id in reversed(range(depth)):
        rounded, mean_in, pre_norm = saved[layer_id]
        d_hidden, d_weights[layer_id], d_pairs[layer_id] = layer_backward(
            d_hidden,
            weights[layer_id],
            norm_params[layer_id],
            rounded,
            mean_in,
            pre_norm,
            boundary[layer_id],
            neighbours[layer_id],
            counts[layer_id],
            layer_id > 0,
        )
    d_first = d_weights[0]
    d_rest = jnp.stack(d_weights[1:])
    d_norms = jnp.stack(d_pairs)
    hid_total = full_first.shape[1]
    g_first, g_rest, g_head = (
        lax.psum_scatter(d_first, "dom", scatter_dimension=1, tiled=True),
        lax.psum_scatter(d_rest, "dom", scatter_dimension=2, tiled=True),
        lax.psum_scatter(d_head, "dom", scatter_dimension=0, tiled=True),
    )
    sq_first = g_first * g_first + SQUARE_EPS
    sq_rest = g_rest * g_rest + SQUARE_EPS
    sq_head = g_head * g_head + SQUARE_EPS
    head_row_new = 0.5 * head_row + 0.5 * jnp.mean(sq_head, axis=1)
    g_norms, g_bias, first_sums, rest_sums, head_sums, head_row_total = lax.psum(
        (
            d_norms,
            d_bias,
            jnp.sum(sq_first, axis=1),
            jnp.sum(sq_rest, axis=2),
            jnp.sum(sq_head, axis=0),
            jnp.sum(head_row_new),
        ),
        "dom",
    )
    first_row_new = 0.5 * first_row + 0.5 * first_sums / hid_total
    first_col_new = 0.5 * first_col + 0.5 * jnp.mean(sq_first, axis=0)
    rest_row_new = 0.5 * rest_row + 0.5 * rest_sums / hid_total
    rest_col_new = 0.5 * rest_col + 0.5 * jnp.mean(sq_rest, axis=1)
    head_col_new = 0.5 * head_col + 0.5 * head_sums / hid_total
    head_row_mean = head_row_total / hid_total
    first_new = factored_step(
        first_weight, g_first, first_row_new, first_col_new, jnp.mean(first_row_new)
    )
    rest_new = factored_step(
        rest_weight, g_rest, rest_row_new, rest_col_new, jnp.mean(rest_row_new, axis=1)
    )
    head_new = factored_step(head_weight, g_head, head_row_new, head_col_new, head_row_mean)
    norm_new, norm_state_new = vector_step(norm_params, g_norms, norm_state)
    bias_new, bias_state_new = vector_step(head_bias, g_bias, bias_state)
    return (
        loss_sum,
        label_count,
        first_new,
        rest_new,
        head_new,
        norm_new,
        bias_new,
        g_first,
        g_rest,
        g_head,
        g_norms,
        g_bias,
        first_row_new,
        first_col_new,
        rest_row_new,
        rest_col_new,
        head_row_new,
        head_col_new,
        norm_state_new,
        bias_state_new,
        first_new.astype(jnp.bfloat16),
        rest_new.astype(jnp.bfloat16),
        head_new.astype(jnp.bfloat16),
        norm_new.astype(jnp.bfloat16),
    )


def solution(mesh):
    placed = (
        P("dom", None),
        P("dom"),
        P("dom"),
        P(None, "dom"),
        P(None, "dom", None),
        P(None, "dom"),
        P(None, "dom"),
        P(None, None, "dom"),
        P("dom", None),
        P(),
        P(),
        P(),
        P("dom"),
        P(),
        P(None, "dom"),
        P("dom"),
        P(),
        P(),
        P(),
    )
    return jax.shard_map(
        on_device,
        mesh=mesh,
        in_specs=placed,
        out_specs=(
            P(),
            P(),
            P(None, "dom"),
            P(None, None, "dom"),
            P("dom", None),
            P(),
            P(),
            P(None, "dom"),
            P(None, None, "dom"),
            P("dom", None),
            P(),
            P(),
            P(),
            P("dom"),
            P(),
            P(None, "dom"),
            P("dom"),
            P(),
            P(),
            P(),
            P(None, "dom"),
            P(None, None, "dom"),
            P("dom", None),
            P(),
        ),
        check_vma=False,
    )
```

profile of v0, /device:TPU:12, one launch (start us, length us, event | category | flops | bytes accessed | tf_op | source)
XLA Modules:
  0.0 2426.4 jit_solution(16949186634642123766)
XLA Ops:
  13.5 32.0 %all_gather.19 = bf16[200,256]{0,1:T(8,128)(2,1)S(1)} all-gather(bf16[200,8]{0,1:T(8,128)(2,1)S(1)} %convert_element_type.116), channel_id=1, replica_groups=mesh['dom'=32] {'dom'}, dimensions={1}, use_global_device_ids=true | all-gather | bytes 105600 | tf_op jit(solution)/shard_map/all_gather | solution.py:117
  50.0 39.5 %all-gather = bf16[4096,100]{1,0:T(8,128)(2,1)S(1)} all-gather(bf16[128,100]{1,0:T(8,128)(2,1)S(1)} %gather_fusion), channel_id=2, replica_groups=mesh['dom'=32] {'dom'}, dimensions={0}, use_global_device_ids=true | all-gather | bytes 844800 | tf_op jit(solution)/shard_map/all_gather | solution.py:31
  101.2 227.3 %gather_fusion.1 = bf16[65536,100]{1,0:T(8,128)(2,1)} fusion(bf16[8192,100]{1,0:T(8,128)(2,1)S(1)} %pad_maximum_fusion.8, s32[65536]{0:T(1024)S(1)} %broadcast_clamp_fusion.2), kind=kCustom, calls=%fused_computation.1 | custom fusion | bytes 26476544 | tf_op jit(solution)/shard_map/gather | solution.py:17
  328.5 8.7 fusion.57
  358.3 39.9 %all_gather.21 = bf16[2,512,256]{1,2,0:T(8,128)(2,1)S(1)} all-gather(bf16[2,512,8]{1,2,0:T(8,128)(2,1)S(1)} %convert_element_type.120), channel_id=1, replica_groups=mesh['dom'=32] {'dom'}, dimensions={2}, use_global_device_ids=true | all-gather | bytes 540672 | tf_op jit(solution)/shard_map/all_gather | solution.py:118
  400.0 10.1 all-gather.6.cloned.1.call-done
  420.5 243.2 %gather_fusion.3 = bf16[65536,256]{1,0:T(8,128)(2,1)} fusion(bf16[8192,256]{1,0:T(8,128)(2,1)} %copy.138, s32[65536]{0:T(1024)S(1)} %broadcast_clamp_fusion.1), kind=kCustom, calls=%fused_computation.3 | custom fusion | bytes 67371008 | tf_op jit(solution)/shard_map/gather | solution.py:17
  663.7 16.7 fusion.2
  680.4 10.1 copy.162
  721.2 31.0 %all_gather.23 = bf16[256,47]{1,0:T(8,128)(2,1)S(1)} all-gather(bf16[8,47]{1,0:T(8,128)(2,1)S(1)} %convert_element_type.125), channel_id=1, replica_groups=mesh['dom'=32] {'dom'}, dimensions={0}, use_global_device_ids=true | all-gather | bytes 24816 | tf_op jit(solution)/shard_map/all_gather | solution.py:119
  767.1 243.2 %gather_fusion.5 = bf16[65536,256]{1,0:T(8,128)(2,1)} fusion(bf16[8192,256]{1,0:T(8,128)(2,1)} %copy.142, s32[65536]{0:T(1024)S(1)} %broadcast_clamp_fusion), kind=kCustom, calls=%fused_computation.5 | custom fusion | bytes 67371008 | tf_op jit(solution)/shard_map/gather | solution.py:17
  1010.3 16.7 fusion
  1027.0 10.1 copy.164
  1045.5 45.2 %psum.57 = f32[]{:T(128)} all-reduce(f32[]{:T(128)} %get-tuple-element.160), channel_id=1, replica_groups=mesh['dom'=32] {'dom'}, use_global_device_ids=true, to_apply=%region_12.13 | all-reduce | flops 1 | bytes 8 | tf_op jit(solution)/shard_map/psum | solution.py:142
  1121.2 22.9 bitcast_multiply_fusion.1
  1144.1 355.9 %scatter_custom_fusion = f32[8192,256]{1,0:T(8,128)} fusion(s32[65536]{0:T(1024)} %bitcast.105, f32[65536,256]{1,0:T(8,128)} %bitcast_multiply_fusion.1, f32[]{:T(128)} %constant.33.clone.1), kind=kCustom, calls=%fused_computation.40 | custom fusion | flops 16777216 | bytes 8389120 | tf_op jit(solution)/shard_map/scatter-add | solution.py:78
  1500.0 8.6 fusion.49
  1514.1 105.8 %reduce-scatter.4.cloned.1.call-done = f32[128,256]{1,0:T(8,128)} async-done(((f32[4096,256]{1,0:T(8,128)}), f32[128,256]{1,0:T(8,128)}) %reduce-scatter.4.cloned.1.call-update) | async-done | bytes 131088 | tf_op jit(solution)/shard_map/reduce_scatter | solution.py:79
  1667.5 23.3 bitcast_multiply_fusion
  1690.8 356.4 %scatter_custom_fusion.2 = f32[8192,256]{1,0:T(8,128)} fusion(s32[65536]{0:T(1024)} %bitcast.106, f32[65536,256]{1,0:T(8,128)} %bitcast_multiply_fusion, f32[]{:T(128)} %constant.33.clone.1), kind=kCustom, calls=%fused_computation.38 | custom fusion | flops 16777216 | bytes 8389120 | tf_op jit(solution)/shard_map/scatter-add | solution.py:78
  2058.1 69.0 %all-reduce.1 = f32[256,47]{1,0:T(8,128)S(1)} all-reduce(f32[256,47]{1,0:T(8,128)S(1)} %fusion.58), channel_id=9, replica_groups=mesh['dom'=32] {'dom'}, use_global_device_ids=true, to_apply=%region_35.36.clone | all-reduce | flops 12032 | bytes 96256
  2128.8 64.0 %reduce-scatter.6.cloned.1.call-done = f32[128,256]{1,0:T(8,128)} async-done(((f32[4096,256]{1,0:T(8,128)}), f32[128,256]{1,0:T(8,128)}) %reduce-scatter.6.cloned.1.call-update) | async-done | bytes 131088 | tf_op jit(solution)/shard_map/reduce_scatter | solution.py:79
  2214.4 128.8 %reduce-scatter.8.cloned.1.call-done = f32[200,8]{0,1:T(8,128)} async-done(((f32[200,256]{0,1:T(8,128)}), f32[200,8]{0,1:T(8,128)}) %reduce-scatter.8.cloned.1.call-update) | async-done | bytes 6416 | tf_op jit(solution)/shard_map/reduce_scatter | solution.py:173
  2344.0 68.3 %all-reduce.2 = (f32[]{:T(128)}, f32[200]{0:T(256)S(1)}, f32[2,512]{1,0:T(2,128)S(1)}, f32[]{:T(128)}, f32[47]{0:T(128)S(1)}, /*index=5*/f32[3,2,256]{2,1,0:T(2,128)S(1)}, f32[47]{0:T(128)S(1)}) all-reduce(f32[]{:T(128)} %get-tuple-element.161, f32[200]{0:T(256)S(1)} %get-tuple-element.163, ...), channel_id=1, replica_groups=mesh['dom'=32] {'dom'}, use_global_device_ids=true, to_apply=%region_10.11 | all-reduce | flops 2856 | bytes 22848 | tf_op jit(solution)/shard_map/psum | solution.py:142
  (300 shorter events, 232.5 us)
Async XLA Ops:
  7.2 403.0 %all-gather.6.cloned.1.call-start = ((), (), s32[]{:S(2)}) async-start(), calls=%async_computation.6 | async-start | bytes 2162688 | tf_op jit(solution)/shard_map/all_gather | solution.py:31
  49.3 288.7 %copy-start.9 = (bf16[4096,100]{1,0:T(8,128)(2,1)}, bf16[4096,100]{1,0:T(8,128)(2,1)S(1)}, u32[]{:S(2)}) copy-start(bf16[4096,100]{1,0:T(8,128)(2,1)S(1)} %copy.133) | copy-start | bytes 2457604
  342.7 350.3 %copy-start.7 = (bf16[4096,256]{0,1:T(8,128)(2,1)}, bf16[4096,256]{0,1:T(8,128)(2,1)S(1)}, u32[]{:S(2)}) copy-start(bf16[4096,256]{0,1:T(8,128)(2,1)S(1)} %multiply_convert_fusion.5) | copy-start | bytes 6291460
  348.9 407.9 %all-gather.8.cloned.1.call-start = ((), (), s32[]{:S(2)}) async-start(), calls=%async_computation.7 | async-start | bytes 2162688 | tf_op jit(solution)/shard_map/all_gather | solution.py:31
  349.2 341.3 %copy-start.37 = (f32[4096]{0:T(1024)}, f32[4096]{0:T(1024)S(1)}, u32[]{:S(2)}) copy-start(f32[4096]{0:T(1024)S(1)} %convert_element_type.118) | copy-start | bytes 49156
  398.2 641.5 %copy-start.20 = (bf16[2,512,256]{1,2,0:T(8,128)(2,1)}, bf16[2,512,256]{1,2,0:T(8,128)(2,1)S(1)}, u32[]{:S(2)}) copy-start(bf16[2,512,256]{1,2,0:T(8,128)(2,1)S(1)} %all_gather.21) | copy-start | bytes 1572868
  703.7 916.2 %reduce-scatter.4.cloned.1.call-start = ((), (), s32[]{:S(2)}) async-start(), calls=%async_computation.3 | async-start | bytes 4325376 | tf_op jit(solution)/shard_map/reduce_scatter | solution.py:79
  1508.7 619.2 %all-reduce.5.cloned.1.call-start = ((), (), s32[]{:S(2)}) async-start(), calls=%async_computation.8 | async-start | bytes 2097152
  1510.6 109.3 %copy-start.65 = (s32[128]{0:T(128)S(1)}, s32[128]{0:T(128)}, u32[]{:S(2)}) copy-start(s32[128]{0:T(128)} %get-tuple-element.219) | copy-start | bytes 1540
  1646.7 546.1 %reduce-scatter.6.cloned.1.call-start = ((), (), s32[]{:S(2)}) async-start(), calls=%async_computation.4 | async-start | bytes 4325376 | tf_op jit(solution)/shard_map/reduce_scatter | solution.py:79
  2055.8 137.0 %copy-start.63 = (s32[128]{0:T(128)S(1)}, s32[128]{0:T(128)}, u32[]{:S(2)}) copy-start(s32[128]{0:T(128)} %get-tuple-element.221) | copy-start | bytes 1540
  2055.8 287.4 %reduce-scatter.8.cloned.1.call-start = ((), (), s32[]{:S(2)}) async-start(), calls=%async_computation.5 | async-start | bytes 270336 | tf_op jit(solution)/shard_map/reduce_scatter | solution.py:173
  2127.2 289.7 %copy-start.50 = (f32[8,47]{1,0:T(8,128)}, f32[8,47]{1,0:T(8,128)S(1)}, u32[]{:S(2)}) copy-start(f32[8,47]{1,0:T(8,128)S(1)} %get-tuple-element.192) | copy-start | bytes 4516
  2127.9 289.0 %copy-start.70 = (f32[8]{0:T(128)}, f32[8]{0:T(128)S(1)}, u32[]{:S(2)}) copy-start(f32[8]{0:T(128)S(1)} %get-tuple-element.191) | copy-start | bytes 100
  2210.4 201.9 %copy-start.67 = (f32[2,512]{1,0:T(2,128)S(1)}, f32[2,512]{1,0:T(2,128)}, u32[]{:S(2)}) copy-start(f32[2,512]{1,0:T(2,128)} %param.32) | copy-start | bytes 12292
  2210.4 202.0 %copy-start.41 = (f32[2,512,8]{1,2,0:T(8,128)S(1)}, f32[2,512,8]{1,2,0:T(8,128)}, u32[]{:S(2)}) copy-start(f32[2,512,8]{1,2,0:T(8,128)} %param.26) | copy-start | bytes 98308
  2210.4 203.4 %copy-start.78 = (f32[8]{0:T(128)S(1)}, f32[8]{0:T(128)}, u32[]{:S(2)}) copy-start(f32[8]{0:T(128)} %param.31) | copy-start | bytes 100
  2210.4 204.0 %copy-start.79 = (f32[47]{0:T(128)S(1)}, f32[47]{0:T(128)}, u32[]{:S(2)}) copy-start(f32[47]{0:T(128)} %param.35) | copy-start | bytes 568
  2210.5 204.0 %copy-start.72 = (f32[200]{0:T(256)S(1)}, f32[200]{0:T(256)}, u32[]{:S(2)}) copy-start(f32[200]{0:T(256)} %param.30) | copy-start | bytes 2404
  2210.5 205.3 %copy-start.74 = (f32[47]{0:T(128)S(1)}, f32[47]{0:T(128)}, u32[]{:S(2)}) copy-start(f32[47]{0:T(128)} %param.37) | copy-start | bytes 568
  2210.5 205.8 %copy-start.46 = (f32[3,2,256]{2,1,0:T(2,128)S(1)}, f32[3,2,256]{2,1,0:T(2,128)}, u32[]{:S(2)}) copy-start(f32[3,2,256]{2,1,0:T(2,128)} %param.28) | copy-start | bytes 18436
  2210.5 205.8 %copy-start.60 = (f32[3,2,256]{2,1,0:T(2,128)S(1)}, f32[3,2,256]{2,1,0:T(2,128)}, u32[]{:S(2)}) copy-start(f32[3,2,256]{2,1,0:T(2,128)} %param.36) | copy-start | bytes 18436
  2210.5 206.4 %copy-start.49 = (f32[8,47]{1,0:T(8,128)S(1)}, f32[8,47]{1,0:T(8,128)}, u32[]{:S(2)}) copy-start(f32[8,47]{1,0:T(8,128)} %param.27) | copy-start | bytes 4516
  2210.5 207.1 %copy-start.45 = (f32[200,8]{0,1:T(8,128)S(1)}, f32[200,8]{0,1:T(8,128)}, u32[]{:S(2)}) copy-start(f32[200,8]{0,1:T(8,128)} %param.25) | copy-start | bytes 19204
  (62 other events, 325.5 us)
Sparse Core Ops, SparseCore 0:
  349.0 61.1 all-gather.5
  703.9 52.8 all-gather.7
  1508.8 111.0 reduce-scatter.3
  1646.8 154.0 all-reduce.4
  2056.0 136.7 reduce-scatter.5
  2213.2 129.9 reduce-scatter.7
where the time goes:
time: 2440 us; the launch traced here: 2430 us
  local copies, waits for them, and re-layouts  853 us (35%)
  other arithmetic  851 us (35%)
  blocking collectives  325 us (13%)
  waiting for transfers between devices  313 us (13%)
  matrix products  65.2 us (3%)
    gather x3, local copies, waits for them, and re-layouts, aggregate(): picked = source[slot_ids]  714 us
    scatter-add x2, other arithmetic, layer_backward(): d_source.at[slot_ids.reshape(-1)].add(spread_out.reshape(-1, feat_width))  712 us
    reduce_scatter x2, waiting for transfers between devices, layer_backward(): lax.psum_scatter(d_source[node_rows:], 'dom', scatter_dimension=0, tiled=...  170 us
    reduce_scatter x1, waiting for transfers between devices, on_device(): lax.psum_scatter(d_first, 'dom', scatter_dimension=1, tiled=True)  129 us
    psum x2, blocking collectives, on_device(): lax.psum((jnp.sum(label_live * (log_total - picked)), jnp.sum(label_live)...  113 us
    unnamed x1, blocking collectives  69 us
  transfers between devices with their start and end apart: 6, of which 5 were waited for; matrix products, arithmetic and copies ran while one was open for 18% of the time, Pallas kernels for 0%

commit v1 on v0

v1 whole, which is shorter than its diff:
```python
import functools

import jax
import jax.numpy as jnp
from jax import lax
from jax.experimental import pallas as pl
from jax.experimental.pallas import tpu as pltpu
from jax.sharding import PartitionSpec as P

LEARN_RATE = 0.03
VECTOR_RATE = 0.25
SQUARE_EPS = 1e-30
NORM_EPS = 1e-05

BF = jnp.bfloat16
F32 = jnp.float32
F8 = jnp.float8_e4m3fn
I32 = jnp.int32

D00 = (((0,), (0,)), ((), ()))
D11 = (((1,), (1,)), ((), ()))
D10 = (((1,), (0,)), ((), ()))

LO = 256
BUILD_NODES = 256
GROUP_NODES = 16
FWD_NODES = 512
BWD_COLS = 1024


def mm(left, right, dims):
    return lax.dot_general(left, right, dims, preferred_element_type=F32)


def iota(shape, dim):
    return lax.broadcasted_iota(I32, shape, dim)


def params():
    return pltpu.CompilerParams(vmem_limit_bytes=56 << 20)


def whole(shape):
    return pl.BlockSpec(shape, lambda i: (0,) * len(shape))


def hop(value, mask, total):
    return lax.ppermute(value, "dom", [(i, i ^ mask) for i in range(total)])


def reverse_bits(value, bits):
    out = 0
    for b in range(bits):
        out = out | (((value >> b) & 1) << (bits - 1 - b))
    return out


def gather_rows(rows, total):
    mask = total // 2
    while mask:
        rows = jnp.concatenate([rows, hop(rows, mask, total)], axis=0)
        mask //= 2
    return rows


def scatter_rows(rows, total):
    mask = 1
    while mask < total:
        half = rows.shape[0] // 2
        rows = rows[:half] + hop(rows[half:], mask, total)
        mask *= 2
    return rows


def sum_all(value, total):
    mask = 1
    while mask < total:
        value = value + hop(value, mask, total)
        mask *= 2
    return value


def build_kernel(me_ref, ids_ref, cnt_ref, loc_ref, bnd_ref, base_ref, low_ref, *, layer, bits, own):
    slots, nodes = ids_ref.shape[1:]
    loc_blocks = loc_ref.shape[1] // LO
    bnd_blocks = bnd_ref.shape[1] // LO
    node_total = loc_ref.shape[1]
    ids = ids_ref[0]
    count = cnt_ref[layer : layer + 1, :]
    table = ids - node_total
    part = reverse_bits((table // own) ^ me_ref[0], bits)
    moved = node_total + part * own + table % own
    ids = jnp.where(ids < node_total, ids, moved)
    ids = jnp.where(iota((slots, nodes), 0) < count, ids, -1)
    high = (ids >> 8).astype(F32).astype(BF)
    low = (ids & 255).astype(F32).astype(BF)
    width = slots * GROUP_NODES
    spread = (iota((slots, width), 0) == iota((slots, width), 1) // GROUP_NODES).astype(F32).astype(BF)
    high_wide = mm(high, spread, D00)
    low_wide = mm(low, spread, D00)
    same = iota((nodes, width), 0) % GROUP_NODES == iota((nodes, width), 1) % GROUP_NODES
    base_ref[...] = jnp.where(same, high_wide, -1.0).astype(BF)
    low_ref[...] = jnp.where(same, low_wide, 0.0)
    low_iota = iota((LO, width), 0).astype(F32).astype(BF)
    one = jnp.ones((), BF)
    zero = jnp.zeros((), BF)

    def chunk(start, groups):
        outs = []
        for g in range(groups):
            r = start + g * GROUP_NODES
            base = base_ref[pl.ds(r, GROUP_NODES), :]
            low_row = jnp.sum(low_ref[pl.ds(r, GROUP_NODES), :], axis=0, keepdims=True).astype(BF)
            right = jnp.where(low_row == low_iota, one, zero)
            left = jnp.concatenate(
                [jnp.where(base == jnp.asarray(h, BF), one, zero) for h in range(loc_blocks + bnd_blocks)], axis=0
            )
            outs.append(mm(left, right, D11))
        for h in range(loc_blocks + bnd_blocks):
            rows = jnp.concatenate([o[h * GROUP_NODES : (h + 1) * GROUP_NODES] for o in outs], axis=0).astype(F8)
            where = pl.ds(start, groups * GROUP_NODES)
            if h < loc_blocks:
                loc_ref[where, h * LO : (h + 1) * LO] = rows
            else:
                b = h - loc_blocks
                bnd_ref[where, b * LO : (b + 1) * LO] = rows

    step = 2 * GROUP_NODES
    if loc_blocks + bnd_blocks <= 32:
        for s in range(nodes // step):
            chunk(s * step, 2)
    else:

        def body(s, carry):
            chunk(pl.multiple_of(s * step, step), 2)
            return carry

        lax.fori_loop(0, nodes // step, body, 0)


def build(me, ids, counts, layer, total, own):
    slots, node_total = ids.shape[1:]
    bnd_total = total * own
    nodes = BUILD_NODES if total <= 32 else 64
    nodes = max(nodes, 128)
    width = slots * GROUP_NODES
    return pl.pallas_call(
        functools.partial(build_kernel, layer=layer, bits=total.bit_length() - 1, own=own),
        grid=(node_total // nodes,),
        in_specs=[
            pl.BlockSpec(memory_space=pltpu.SMEM),
            pl.BlockSpec((1, slots, nodes), lambda i: (layer, 0, i)),
            pl.BlockSpec((counts.shape[0], nodes), lambda i: (0, i)),
        ],
        out_specs=[
            pl.BlockSpec((nodes, node_total), lambda i: (i, 0)),
            pl.BlockSpec((nodes, bnd_total), lambda i: (i, 0)),
        ],
        out_shape=[
            jax.ShapeDtypeStruct((node_total, node_total), F8),
            jax.ShapeDtypeStruct((node_total, bnd_total), F8),
        ],
        scratch_shapes=[pltpu.VMEM((nodes, width), BF), pltpu.VMEM((nodes, width), F32)],
        compiler_params=params(),
        cost_estimate=pl.CostEstimate(
            flops=2 * node_total * (node_total + bnd_total) * 256,
            bytes_accessed=node_total * (node_total + bnd_total),
            transcendentals=0,
        ),
        name="build_counts",
    )(me, ids, counts)


def local_kernel(a_ref, table_ref, out_ref):
    out_ref[...] = mm(a_ref[...].astype(BF), table_ref[...], D10)


def local_sum(a_loc, table):
    node_total, feat = table.shape
    return pl.pallas_call(
        local_kernel,
        grid=(node_total // FWD_NODES,),
        in_specs=[
            pl.BlockSpec((FWD_NODES, node_total), lambda i: (i, 0)),
            whole((node_total, feat)),
        ],
        out_specs=pl.BlockSpec((FWD_NODES, feat), lambda i: (i, 0)),
        out_shape=jax.ShapeDtypeStruct((node_total, feat), F32),
        compiler_params=params(),
        cost_estimate=pl.CostEstimate(
            flops=2 * node_total * node_total * 256, bytes_accessed=node_total * node_total, transcendentals=0
        ),
        name="local_sum",
    )(a_loc, table)


def columns(rows, width):
    nodes = rows[0].shape[1]
    pick = iota((16, nodes), 0)
    stacked = jnp.zeros((16, nodes), F32)
    for r, row in enumerate(rows):
        stacked = jnp.where(pick == r, row.astype(F32), stacked)
    stacked = stacked.astype(BF)
    outs = []
    for r in range(len(rows)):
        take = (iota((16, width), 0) == r).astype(F32).astype(BF)
        outs.append(mm(stacked, take, D00))
    return outs


def normalise(pre):
    centre = pre - jnp.mean(pre, axis=1, keepdims=True)
    inv = lax.rsqrt(jnp.mean(centre * centre, axis=1, keepdims=True) + NORM_EPS)
    return centre * inv, inv


def row_hot(brow, start, nodes):
    return (iota((nodes, brow.shape[1]), 0) + start == brow).astype(F32).astype(BF)


def forward_block(a_ref, shared_ref, part_ref, hid_ref, cnt_ref, self_ref, neigh_ref, norm_ref, layer):
    feat = hid_ref.shape[1]
    (count,) = columns([cnt_ref[layer : layer + 1, :]], feat)
    total = part_ref[...] + mm(a_ref[...].astype(BF), shared_ref[...], D10)
    agg = (total / count).astype(BF)
    pre = mm(hid_ref[...], self_ref[...], D11) + mm(agg, neigh_ref[...], D11)
    unit, inv = normalise(pre)
    y = unit * norm_ref[layer, 0:1, :] + norm_ref[layer, 1:2, :]
    return agg, pre, unit, inv, y, count


def layer_kernel(
    a_ref, shared_ref, part_ref, hid_ref, cnt_ref, self_ref, neigh_ref, norm_ref, brow_ref,
    next_ref, agg_ref, pre_ref, pub_ref, acc_ref, *, layer
):
    step = pl.program_id(0)
    agg, pre, _, _, y, _ = forward_block(
        a_ref, shared_ref, part_ref, hid_ref, cnt_ref, self_ref, neigh_ref, norm_ref, layer
    )
    nodes = hid_ref.shape[0]
    agg_ref[...] = agg
    pre_ref[...] = pre
    new = (y * jax.nn.sigmoid(y)).astype(BF)
    next_ref[...] = new
    hot = row_hot(brow_ref[layer + 1 : layer + 2, :], step * nodes, nodes)

    @pl.when(step == 0)
    def _():
        acc_ref[...] = jnp.zeros_like(acc_ref)

    acc_ref[...] += mm(hot, new, D00)

    @pl.when(step == pl.num_programs(0) - 1)
    def _():
        pub_ref[...] = acc_ref[...].astype(BF)


def forward_specs(node_total, bnd_total, feat, hid, depth, own):
    return [
        pl.BlockSpec((FWD_NODES, bnd_total), lambda i: (i, 0)),
        whole((bnd_total, feat)),
        pl.BlockSpec((FWD_NODES, feat), lambda i: (i, 0)),
        pl.BlockSpec((FWD_NODES, feat), lambda i: (i, 0)),
        pl.BlockSpec((depth, FWD_NODES), lambda i: (0, i)),
        whole((hid, feat)),
        whole((hid, feat)),
        whole((depth, 2, hid)),
    ]


def rows_spec(width):
    return pl.BlockSpec((FWD_NODES, width), lambda i: (i, 0))


def layer_forward(layer, a_bnd, shared, part, hidden, counts, w_self, w_neigh, norms, boundary):
    node_total, feat = hidden.shape
    bnd_total = shared.shape[0]
    hid = w_self.shape[0]
    depth, own = boundary.shape
    return pl.pallas_call(
        functools.partial(layer_kernel, layer=layer),
        grid=(node_total // FWD_NODES,),
        in_specs=forward_specs(node_total, bnd_total, feat, hid, depth, own) + [whole((depth, own))],
        out_specs=[rows_spec(hid), rows_spec(feat), rows_spec(hid), whole((own, hid))],
        out_shape=[
            jax.ShapeDtypeStruct((node_total, hid), BF),
            jax.ShapeDtypeStruct((node_total, feat), BF),
            jax.ShapeDtypeStruct((node_total, hid), F32),
            jax.ShapeDtypeStruct((own, hid), BF),
        ],
        scratch_shapes=[pltpu.VMEM((own, hid), F32)],
        compiler_params=params(),
        cost_estimate=pl.CostEstimate(
            flops=2 * node_total * (bnd_total + 1024) * 256,
            bytes_accessed=node_total * (bnd_total + 4096),
            transcendentals=0,
        ),
        name="layer_step",
    )(a_bnd, shared, part, hidden, counts, w_self, w_neigh, norms, boundary)


def backward_block(d_hidden, unit, inv, y, gain):
    sig = jax.nn.sigmoid(y)
    d_out = d_hidden * sig * (1.0 + y * (1.0 - sig))
    d_gain = jnp.sum(d_out * unit, axis=0, keepdims=True)
    d_shift = jnp.sum(d_out, axis=0, keepdims=True)
    d_unit = d_out * gain
    d_pre = inv * (
        d_unit
        - jnp.mean(d_unit, axis=1, keepdims=True)
        - unit * jnp.mean(d_unit * unit, axis=1, keepdims=True)
    )
    return d_pre.astype(BF), d_gain, d_shift


def add_weight_sums(dw_ref, dnorm_ref, d_pre, perm, hidden, agg, d_gain, d_shift, step):
    @pl.when(step == 0)
    def _():
        dw_ref[...] = jnp.zeros_like(dw_ref)
        dnorm_ref[...] = jnp.zeros_like(dnorm_ref)

    feat = hidden.shape[1]
    offset = dw_ref.shape[1] // 2
    moved = mm(d_pre, perm, D10).astype(BF)
    dw_ref[:, 0:feat] += mm(moved, hidden, D00)
    dw_ref[:, offset : offset + feat] += mm(moved, agg, D00)
    dnorm_ref[0:1, :] += d_gain
    dnorm_ref[1:2, :] += d_shift


def top_kernel(
    lc_ref, a_ref, shared_ref, part_ref, hid_ref, cnt_ref, self_ref, neigh_ref, norm_ref,
    lab_ref, mask_ref, head_ref, bias_ref, perm_ref,
    ds_ref, da_ref, dw_ref, dnorm_ref, dhead_ref, dbias_ref, loss_ref, *, layer
):
    step = pl.program_id(0)
    agg, _, unit, inv, y, count = forward_block(
        a_ref, shared_ref, part_ref, hid_ref, cnt_ref, self_ref, neigh_ref, norm_ref, layer
    )
    classes = head_ref.shape[1]
    top = (y * jax.nn.sigmoid(y)).astype(BF)
    logits = mm(top, head_ref[...], D10) + bias_ref[...]
    label, live = columns([lab_ref[...], mask_ref[...]], classes)
    peak = jnp.max(logits, axis=1, keepdims=True)
    log_total = peak + jnp.log(jnp.sum(jnp.exp(logits - peak), axis=1, keepdims=True))
    hot = label == iota(label.shape, 1).astype(F32)
    part_loss = jnp.sum(jnp.where(hot, live * (log_total - logits), 0.0), axis=0, keepdims=True)
    probs = jnp.exp(logits - log_total)
    d_logits = ((probs - hot.astype(F32)) * live / lc_ref[0]).astype(BF)
    perm = perm_ref[...]
    moved_top = mm(top, perm, D10).astype(BF)

    @pl.when(step == 0)
    def _():
        dhead_ref[...] = jnp.zeros_like(dhead_ref)
        dbias_ref[...] = jnp.zeros_like(dbias_ref)
        loss_ref[...] = jnp.zeros_like(loss_ref)

    loss_ref[...] += part_loss
    dbias_ref[...] += jnp.sum(d_logits.astype(F32), axis=0, keepdims=True)
    dhead_ref[...] += mm(moved_top, d_logits, D00)
    d_hidden = mm(d_logits, head_ref[...], D11)
    d_pre, d_gain, d_shift = backward_block(d_hidden, unit, inv, y, norm_ref[layer, 0:1, :])
    add_weight_sums(dw_ref, dnorm_ref, d_pre, perm, hid_ref[...], agg, d_gain, d_shift, step)
    ds_ref[...] = mm(d_pre, self_ref[...], D10)
    da_ref[...] = (mm(d_pre, neigh_ref[...], D10) / count).astype(BF)


def top_layer(layer, label_count, a_bnd, shared, part, hidden, counts, w_self, w_neigh, norms, labels, live, head, bias, perm):
    node_total, feat = hidden.shape
    bnd_total = shared.shape[0]
    hid = w_self.shape[0]
    depth = norms.shape[0]
    classes = head.shape[1]
    row = pl.BlockSpec((1, FWD_NODES), lambda i: (0, i))
    return pl.pallas_call(
        functools.partial(top_kernel, layer=layer),
        grid=(node_total // FWD_NODES,),
        in_specs=[pl.BlockSpec(memory_space=pltpu.SMEM)]
        + forward_specs(node_total, bnd_total, feat, hid, depth, 0)
        + [row, row, whole((hid, classes)), whole((1, classes)), whole((hid, hid))],
        out_specs=[
            rows_spec(feat),
            rows_spec(feat),
            whole((hid, 2 * hid)),
            whole((2, hid)),
            whole((hid, classes)),
            whole((1, classes)),
            whole((1, classes)),
        ],
        out_shape=[
            jax.ShapeDtypeStruct((node_total, feat), F32),
            jax.ShapeDtypeStruct((node_total, feat), BF),
            jax.ShapeDtypeStruct((hid, 2 * hid), F32),
            jax.ShapeDtypeStruct((2, hid), F32),
            jax.ShapeDtypeStruct((hid, classes), F32),
            jax.ShapeDtypeStruct((1, classes), F32),
            jax.ShapeDtypeStruct((1, classes), F32),
        ],
        compiler_params=params(),
        cost_estimate=pl.CostEstimate(
            flops=2 * node_total * (bnd_total + 3072) * 256,
            bytes_accessed=node_total * (bnd_total + 4096),
            transcendentals=0,
        ),
        name="top_step",
    )(label_count, a_bnd, shared, part, hidden, counts, w_self, w_neigh, norms, labels, live, head, bias, perm)


def lower_kernel(
    dh_ref, dshared_ref, brow_ref, pre_ref, hid_ref, agg_ref, cnt_ref, norm_ref, perm_ref, self_ref, neigh_ref,
    *outs, layer
):
    step = pl.program_id(0)
    nodes = dh_ref.shape[0]
    hot = row_hot(brow_ref[layer + 1 : layer + 2, :], step * nodes, nodes)
    shared = dshared_ref[...]
    shared_top = shared.astype(BF)
    shared_rest = (shared - shared_top.astype(F32)).astype(BF)
    d_hidden = dh_ref[...] + mm(hot, shared_top, D10) + mm(hot, shared_rest, D10)
    unit, inv = normalise(pre_ref[...])
    gain = norm_ref[layer, 0:1, :]
    y = unit * gain + norm_ref[layer, 1:2, :]
    d_pre, d_gain, d_shift = backward_block(d_hidden, unit, inv, y, gain)
    dw_ref, dnorm_ref = outs[0], outs[1]
    add_weight_sums(dw_ref, dnorm_ref, d_pre, perm_ref[...], hid_ref[...], agg_ref[...], d_gain, d_shift, step)
    if len(outs) > 2:
        (count,) = columns([cnt_ref[layer : layer + 1, :]], hid_ref.shape[1])
        outs[2][...] = mm(d_pre, self_ref[...], D10)
        outs[3][...] = (mm(d_pre, neigh_ref[...], D10) / count).astype(BF)


def layer_backward(layer, d_hidden, d_shared, boundary, pre, hidden, agg, counts, norms, perm, w_self, w_neigh):
    node_total, hid = d_hidden.shape
    feat = hidden.shape[1]
    depth, own = boundary.shape
    wide = 2 * (-(-feat // 128) * 128)
    out_specs = [whole((hid, wide)), whole((2, hid))]
    out_shape = [jax.ShapeDtypeStruct((hid, wide), F32), jax.ShapeDtypeStruct((2, hid), F32)]
    if layer:
        out_specs += [rows_spec(feat), rows_spec(feat)]
        out_shape += [
            jax.ShapeDtypeStruct((node_total, feat), F32),
            jax.ShapeDtypeStruct((node_total, feat), BF),
        ]
    return pl.pallas_call(
        functools.partial(lower_kernel, layer=layer),
        grid=(node_total // FWD_NODES,),
        in_specs=[
            rows_spec(hid),
            whole((own, hid)),
            whole((depth, own)),
            rows_spec(hid),
            rows_spec(feat),
            rows_spec(feat),
            pl.BlockSpec((depth, FWD_NODES), lambda i: (0, i)),
            whole((depth, 2, hid)),
            whole((hid, hid)),
            whole((hid, feat)),
            whole((hid, feat)),
        ],
        out_specs=out_specs,
        out_shape=out_shape,
        compiler_params=params(),
        cost_estimate=pl.CostEstimate(
            flops=2 * node_total * 2048 * 256, bytes_accessed=node_total * 6144, transcendentals=0
        ),
        name="lower_step",
    )(d_hidden, d_shared, boundary, pre, hidden, agg, counts, norms, perm, w_self, w_neigh)


def spread_kernel(a_ref, d_ref, *refs):
    total = mm(a_ref[...].astype(BF), d_ref[...], D00)
    if len(refs) > 1:
        total = total + refs[0][...]
    refs[-1][...] = total.astype(refs[-1].dtype)


def spread(a, d_rows, extra, kind, name):
    node_total, cols = a.shape
    feat = d_rows.shape[1]
    block = pl.BlockSpec((BWD_COLS, feat), lambda i: (i, 0))
    return pl.pallas_call(
        spread_kernel,
        grid=(cols // BWD_COLS,),
        in_specs=[pl.BlockSpec((node_total, BWD_COLS), lambda i: (0, i)), whole((node_total, feat))]
        + [block] * len(extra),
        out_specs=block,
        out_shape=jax.ShapeDtypeStruct((cols, feat), kind),
        compiler_params=params(),
        cost_estimate=pl.CostEstimate(
            flops=2 * node_total * cols * 256, bytes_accessed=node_total * cols, transcendentals=0
        ),
        name=name,
    )(a, d_rows, *extra)


def factored_step(weight, gradient, row_new, col_new, row_mean):
    estimate = row_new[..., None, :] * col_new[..., :, None] / row_mean[..., None, None]
    return weight - LEARN_RATE * gradient * lax.rsqrt(estimate)


def vector_step(param, gradient, state):
    state_new = 0.5 * state + 0.5 * (gradient * gradient + SQUARE_EPS)
    return (param - VECTOR_RATE * gradient * lax.rsqrt(state_new), state_new)


def on_device(
    features,
    labels,
    train_mask,
    boundary,
    neighbours,
    counts,
    first_weight,
    rest_weight,
    head_weight,
    norm_params,
    head_bias,
    first_row,
    first_col,
    rest_row,
    rest_col,
    head_row,
    head_col,
    norm_state,
    bias_state,
    *,
    total,
):
    bits = total.bit_length() - 1
    me = lax.axis_index("dom").astype(I32)
    me_ref = me[None]
    depth = norm_params.shape[0]
    own = boundary.shape[1]
    node_total, f_in = features.shape
    hid = norm_params.shape[2]
    classes = head_bias.shape[0]
    cols_own = hid // total

    first_t = first_weight.T
    rest_t = jnp.swapaxes(rest_weight, 1, 2)
    ids = jnp.swapaxes(neighbours, 1, 2)

    label_count = sum_all(jnp.sum(train_mask.astype(F32), keepdims=True).reshape(1, 1), total).reshape(1)

    col = jnp.arange(hid, dtype=I32)
    place = reverse_bits((col // cols_own) ^ me, bits) * cols_own + col % cols_own
    perm = (place[:, None] == jnp.arange(hid, dtype=I32)[None, :]).astype(BF)

    packed = jnp.concatenate(
        [first_t.astype(BF)] + [rest_t[k].astype(BF) for k in range(depth - 1)] + [head_weight.astype(BF)], axis=1
    )
    packed = mm(perm, gather_rows(packed, total), D10).astype(BF)
    first_full = packed[:, : 2 * f_in]
    at = 2 * f_in
    weights = [(first_full[:, :f_in], first_full[:, f_in:])]
    for _ in range(depth - 1):
        weights.append((packed[:, at : at + hid], packed[:, at + hid : at + 2 * hid]))
        at += 2 * hid
    head = packed[:, at:]

    hidden = features.astype(BF)
    published = hidden[boundary[0]]
    saved = []
    for layer in range(depth):
        shared = gather_rows(published, total)
        a_loc, a_bnd = build(me_ref, ids, counts, layer, total, own)
        part = local_sum(a_loc, hidden)
        w_self, w_neigh = weights[layer]
        if layer < depth - 1:
            new, agg, pre, published = layer_forward(
                layer, a_bnd, shared, part, hidden, counts, w_self, w_neigh, norm_params, boundary
            )
            saved.append((a_loc, a_bnd, hidden, agg, pre))
            hidden = new
    ds, da, dw, dnorm, dhead, dbias, loss = top_layer(
        depth - 1, label_count, a_bnd, shared, part, hidden, counts, w_self, w_neigh, norm_params,
        labels[None], train_mask[None], head, head_bias[None], perm,
    )
    d_weights = [None] * depth
    d_norms = [None] * depth
    d_weights[-1], d_norms[-1] = dw, dnorm
    for layer in reversed(range(depth - 1)):
        d_far = spread(a_bnd, da, (), BF, "spread_far")
        d_near = spread(a_loc, da, (ds,), F32, "spread_near")
        d_shared = scatter_rows(d_far, total).astype(F32)
        a_loc, a_bnd, hidden, agg, pre = saved[layer]
        w_self, w_neigh = weights[layer]
        outs = layer_backward(
            layer, d_near, d_shared, boundary, pre, hidden, agg, counts, norm_params, perm, w_self, w_neigh
        )
        d_weights[layer], d_norms[layer] = outs[0], outs[1]
        if layer:
            ds, da = outs[2:]

    g_head = scatter_rows(dhead, total)
    g_rest = jnp.stack([scatter_rows(d_weights[k], total) for k in range(1, depth)])
    g_wide = scatter_rows(d_weights[0], total)
    half = g_wide.shape[1] // 2
    g_first = jnp.concatenate([g_wide[:, :f_in], g_wide[:, half : half + f_in]], axis=1)

    sq_first = g_first * g_first + SQUARE_EPS
    sq_rest = g_rest * g_rest + SQUARE_EPS
    sq_head = g_head * g_head + SQUARE_EPS
    head_row_new = 0.5 * head_row + 0.5 * jnp.mean(sq_head, axis=1)
    pieces = [
        jnp.stack(d_norms).reshape(-1),
        dbias.reshape(-1),
        jnp.sum(sq_first, axis=0),
        jnp.sum(sq_rest, axis=1).reshape(-1),
        jnp.sum(sq_head, axis=0),
        jnp.sum(head_row_new, keepdims=True),
        jnp.sum(loss, keepdims=True).reshape(1),
    ]
    sums = sum_all(jnp.concatenate(pieces), total)
    parts = []
    at = 0
    for piece in pieces:
        parts.append(sums[at : at + piece.shape[0]])
        at += piece.shape[0]
    g_norms = parts[0].reshape(norm_params.shape)
    g_bias = parts[1]
    first_sums = parts[2]
    rest_sums = parts[3].reshape(rest_row.shape)
    head_sums = parts[4]
    head_row_mean = parts[5][0] / hid
    loss_sum = parts[6][0]

    first_row_new = 0.5 * first_row + 0.5 * first_sums / hid
    first_col_new = 0.5 * first_col + 0.5 * jnp.mean(sq_first, axis=1)
    rest_row_new = 0.5 * rest_row + 0.5 * rest_sums / hid
    rest_col_new = 0.5 * rest_col + 0.5 * jnp.mean(sq_rest, axis=2)
    head_col_new = 0.5 * head_col + 0.5 * head_sums / hid
    first_new = factored_step(first_t, g_first, first_row_new, first_col_new, jnp.mean(first_row_new))
    rest_new = factored_step(rest_t, g_rest, rest_row_new, rest_col_new, jnp.mean(rest_row_new, axis=1))
    head_new = head_weight - LEARN_RATE * g_head * lax.rsqrt(
        head_row_new[:, None] * head_col_new[None, :] / head_row_mean
    )
    norm_new, norm_state_new = vector_step(norm_params, g_norms, norm_state)
    bias_new, bias_state_new = vector_step(head_bias, g_bias, bias_state)
    first_new = first_new.T
    rest_new = jnp.swapaxes(rest_new, 1, 2)
    return (
        loss_sum,
        label_count[0],
        first_new,
        rest_new,
        head_new,
        norm_new,
        bias_new,
        g_first.T,
        jnp.swapaxes(g_rest, 1, 2),
        g_head,
        g_norms,
        g_bias,
        first_row_new,
        first_col_new,
        rest_row_new,
        rest_col_new,
        head_row_new,
        head_col_new,
        norm_state_new,
        bias_state_new,
        first_new.astype(BF),
        rest_new.astype(BF),
        head_new.astype(BF),
        norm_new.astype(BF),
    )


def solution(mesh):
    placed = (
        P("dom", None),
        P("dom"),
        P("dom"),
        P(None, "dom"),
        P(None, "dom", None),
        P(None, "dom"),
        P(None, "dom"),
        P(None, None, "dom"),
        P("dom", None),
        P(),
        P(),
        P(),
        P("dom"),
        P(),
        P(None, "dom"),
        P("dom"),
        P(),
        P(),
        P(),
    )
    return jax.shard_map(
        functools.partial(on_device, total=mesh.shape["dom"]),
        mesh=mesh,
        in_specs=placed,
        out_specs=(
            P(),
            P(),
            P(None, "dom"),
            P(None, None, "dom"),
            P("dom", None),
            P(),
            P(),
            P(None, "dom"),
            P(None, None, "dom"),
            P("dom", None),
            P(),
            P(),
            P(),
            P("dom"),
            P(),
            P(None, "dom"),
            P("dom"),
            P(),
            P(),
            P(),
            P(None, "dom"),
            P(None, None, "dom"),
            P("dom", None),
            P(),
        ),
        check_vma=False,
    )
```

time: 2440 us -> 537 us (0.22)
  local copies, waits for them, and re-layouts: 853 us -> 17.9 us
  other arithmetic: 851 us -> 19.9 us
  blocking collectives: 325 us -> 0 us
  Pallas kernels: 0 us -> 291 us
  waiting for transfers between devices: 313 us -> 138 us
  matrix products: 65.2 us -> 0.38 us
  starting transfers between devices: 1.33 us -> 58 us
    scatter-add x4 -> x0, other arithmetic: 724 us -> none  [the longest x2 712 us: layer_backward(): d_source.at[slot_ids.reshape(-1)].add(spread_out.reshape(-1, feat_width))]
    gather x8 -> x1, local copies, waits for them, and re-layouts: 721 us -> 0.71 us  [on_device(): published = hidden[boundary[0]]]
    reduce_scatter x3 -> x0, waiting for transfers between devices: 299 us -> none  [the longest x2 170 us: layer_backward(): lax.psum_scatter(d_source[node_rows:], 'dom', scatter_dimension=0, tiled=...]
    pallas_call x0 -> x15, Pallas kernels: none -> 291 us  [the longest x3 80.1 us: build(): pl.pallas_call(functools.partial(build_kernel, layer=layer, bits=total.bi...]
    all_gather x4 -> x0, blocking collectives: 142 us -> none  [the longest x1 39.9 us: on_device(): lax.all_gather(rest_weight.astype(jnp.bfloat16), 'dom', axis=2, tiled=True)]
    ppermute x0 -> x60, waiting for transfers between devices: none -> 138 us  [hop(): return lax.ppermute(value, 'dom', [(i, i ^ mask) for i in range(total)])]
    psum x2 -> x0, blocking collectives: 113 us -> none  [on_device(): lax.psum((jnp.sum(label_live * (log_total - picked)), jnp.sum(label_live)...]
    unnamed x1 -> x0, blocking collectives: 69 us -> none
  transfers between devices with their start and end apart: 6 -> 60, of which waited for: 5 -> 42; matrix products, arithmetic and copies ran while one was open for 18% -> 3% of each run, Pallas kernels for 0% -> 36%
where the time goes in v1:
time: 537 us; the launch traced here: 533 us
  Pallas kernels  291 us (54%)
  waiting for transfers between devices  138 us (26%)
  starting transfers between devices  58 us (11%)
  other arithmetic  19.9 us (4%)
  local copies, waits for them, and re-layouts  17.9 us (3%)
  between operations  7.51 us (1%)
    ppermute x60, waiting for transfers between devices, hop(): return lax.ppermute(value, 'dom', [(i, i ^ mask) for i in range(total)])  138 us
    pallas_call x3, Pallas kernels, build(): pl.pallas_call(functools.partial(build_kernel, layer=layer, bits=total.bi...  80.1 us
    ppermute x60, starting transfers between devices, hop(): return lax.ppermute(value, 'dom', [(i, i ^ mask) for i in range(total)])  58 us
    pallas_call x4, Pallas kernels, spread(): pl.pallas_call(spread_kernel, grid=(cols // BWD_COLS,), in_specs=[pl.Bloc...  55.2 us
    pallas_call x3, Pallas kernels, local_sum(): pl.pallas_call(local_kernel, grid=(node_total // FWD_NODES,), in_specs=[p...  44.3 us
    pallas_call x2, Pallas kernels, layer_forward(): pl.pallas_call(functools.partial(layer_kernel, layer=layer), grid=(node_t...  42.7 us
    pallas_call x1, Pallas kernels, top_layer(): pl.pallas_call(functools.partial(top_kernel, layer=layer), grid=(node_tot...  40.8 us
    pallas_call x2, Pallas kernels, layer_backward(): pl.pallas_call(functools.partial(lower_kernel, layer=layer), grid=(node_t...  27.5 us
  transfers between devices with their start and end apart: 60, of which 42 were waited for; matrix products, arithmetic and copies ran while one was open for 3% of the time, Pallas kernels for 36%

profile of v1, /device:TPU:12, one launch (start us, length us, event | category | flops | bytes accessed | tf_op | source)
XLA Modules:
  0.0 532.6 jit_solution(387123697841379646)
XLA Ops:
  9.8 26.6 %build_counts.5 = (f8e4m3fn[4096,4096]{1,0:T(32,128)(4,1)}, f8e4m3fn[4096,4096]{1,0:T(32,128)(4,1)}) custom-call(s32[1]{0:T(128)} %bitcast.me_ref, s32[3,16,4096]{2,1,0:T(8,128)} %bitcast.63, s32[3,4096]{1,0:T(4,128)} %cnt_ref.15), custom_call_target="tpu_custom_call" | custom-call | flops 17179869184 | bytes 33554432 | tf_op jit(solution)/shard_map/build_counts/pallas_call | solution.py:147
  36.4 14.3 %local_sum.3.part_ref = f32[4096,100]{1,0:T(8,128)} custom-call(f8e4m3fn[4096,4096]{1,0:T(32,128)(4,1)} %get-tuple-element.56.a_ref, bf16[4096,100]{1,0:T(8,128)(2,1)} %copy-done.2), custom_call_target="tpu_custom_call" | custom-call | flops 8589934592 | bytes 16777216 | tf_op jit(solution)/shard_map/local_sum/pallas_call | solution.py:180
  71.2 20.7 %layer_step.2 = (bf16[4096,256]{1,0:T(8,128)(2,1)}, bf16[4096,100]{1,0:T(8,128)(2,1)}, f32[4096,256]{1,0:T(8,128)}, bf16[128,256]{1,0:T(8,128)(2,1)}) custom-call(f8e4m3fn[4096,4096]{1,0:T(32,128)(4,1)} %get-tuple-element.55.a_ref, bf16[4096,100]{1,0:T(8,128)(2,1)} %copy-done.25, f32[4096,100]{1,0:T(8,128)} %local_sum.3.part_ref, ...), custom_call_target="tpu_custom_call" | custom-call | flops 10737418240 | bytes 33554432 | tf_op jit(solution)/shard_map/layer_step/pallas_call | solution.py:280
  106.3 6.7 %collective-permute-done.17 = bf16[512,256]{1,0:T(8,128)(2,1)S(1)} collective-permute-done((bf16[512,256]{1,0:T(8,128)(2,1)S(1)}, bf16[512,256]{1,0:T(8,128)(2,1)S(1)}, u32[]{:S(2)}, u32[]{:S(2)}) %collective-permute-start.17) | collective-permute-done | bytes 262176 | tf_op jit(solution)/shard_map/ppermute | solution.py:48
  116.6 9.6 %collective-permute-done.18 = bf16[1024,256]{1,0:T(8,128)(2,1)S(1)} collective-permute-done((bf16[1024,256]{1,0:T(8,128)(2,1)S(1)}, bf16[1024,256]{1,0:T(8,128)(2,1)S(1)}, u32[]{:S(2)}, u32[]{:S(2)}) %collective-permute-start.18) | collective-permute-done | bytes 524320 | tf_op jit(solution)/shard_map/ppermute | solution.py:48
  126.3 26.7 %build_counts.3 = (f8e4m3fn[4096,4096]{1,0:T(32,128)(4,1)}, f8e4m3fn[4096,4096]{1,0:T(32,128)(4,1)}) custom-call(s32[1]{0:T(128)} %bitcast.me_ref, s32[3,16,4096]{2,1,0:T(8,128)} %bitcast.64, s32[3,4096]{1,0:T(4,128)} %cnt_ref.15), custom_call_target="tpu_custom_call" | custom-call | flops 17179869184 | bytes 33554432 | tf_op jit(solution)/shard_map/build_counts/pallas_call | solution.py:147
  154.0 15.0 %local_sum.4.part_ref = f32[4096,256]{1,0:T(8,128)} custom-call(f8e4m3fn[4096,4096]{1,0:T(32,128)(4,1)} %get-tuple-element.51.a_ref, bf16[4096,256]{1,0:T(8,128)(2,1)} %get-tuple-element.58.table_ref.hid_ref), custom_call_target="tpu_custom_call" | custom-call | flops 8589934592 | bytes 16777216 | tf_op jit(solution)/shard_map/local_sum/pallas_call | solution.py:180
  170.4 22.0 %layer_step.3 = (bf16[4096,256]{1,0:T(8,128)(2,1)}, bf16[4096,256]{1,0:T(8,128)(2,1)}, f32[4096,256]{1,0:T(8,128)}, bf16[128,256]{1,0:T(8,128)(2,1)}) custom-call(f8e4m3fn[4096,4096]{1,0:T(32,128)(4,1)} %get-tuple-element.54.a_ref, bf16[4096,256]{1,0:T(8,128)(2,1)} %copy-done.18, f32[4096,256]{1,0:T(8,128)} %local_sum.4.part_ref, ...), custom_call_target="tpu_custom_call" | custom-call | flops 10737418240 | bytes 33554432 | tf_op jit(solution)/shard_map/layer_step/pallas_call | solution.py:280
  192.5 5.7 %collective-permute-done.20 = bf16[128,256]{1,0:T(8,128)(2,1)S(1)} collective-permute-done((bf16[128,256]{1,0:T(8,128)(2,1)}, bf16[128,256]{1,0:T(8,128)(2,1)S(1)}, u32[]{:S(2)}, u32[]{:S(2)}) %collective-permute-start.20) | collective-permute-done | bytes 65568 | tf_op jit(solution)/shard_map/ppermute | solution.py:48
  206.8 6.3 %collective-permute-done.22 = bf16[512,256]{1,0:T(8,128)(2,1)S(1)} collective-permute-done((bf16[512,256]{1,0:T(8,128)(2,1)S(1)}, bf16[512,256]{1,0:T(8,128)(2,1)S(1)}, u32[]{:S(2)}, u32[]{:S(2)}) %collective-permute-start.22) | collective-permute-done | bytes 262176 | tf_op jit(solution)/shard_map/ppermute | solution.py:48
  217.3 8.9 %collective-permute-done.23 = bf16[1024,256]{1,0:T(8,128)(2,1)S(1)} collective-permute-done((bf16[1024,256]{1,0:T(8,128)(2,1)S(1)}, bf16[1024,256]{1,0:T(8,128)(2,1)S(1)}, u32[]{:S(2)}, u32[]{:S(2)}) %collective-permute-start.23) | collective-permute-done | bytes 524320 | tf_op jit(solution)/shard_map/ppermute | solution.py:48
  226.3 26.8 %build_counts.4 = (f8e4m3fn[4096,4096]{1,0:T(32,128)(4,1)}, f8e4m3fn[4096,4096]{1,0:T(32,128)(4,1)}) custom-call(s32[1]{0:T(128)} %bitcast.me_ref, s32[3,16,4096]{2,1,0:T(8,128)} %bitcast.65, s32[3,4096]{1,0:T(4,128)} %cnt_ref.15), custom_call_target="tpu_custom_call" | custom-call | flops 17179869184 | bytes 33554432 | tf_op jit(solution)/shard_map/build_counts/pallas_call | solution.py:147
  273.9 15.0 %local_sum.5.part_ref = f32[4096,256]{1,0:T(8,128)} custom-call(f8e4m3fn[4096,4096]{1,0:T(32,128)(4,1)} %get-tuple-element.52.a_ref, bf16[4096,256]{1,0:T(8,128)(2,1)} %get-tuple-element.60.table_ref.hid_ref), custom_call_target="tpu_custom_call" | custom-call | flops 8589934592 | bytes 16777216 | tf_op jit(solution)/shard_map/local_sum/pallas_call | solution.py:180
  290.3 40.8 %top_step.1 = (f32[4096,256]{1,0:T(8,128)}, bf16[4096,256]{1,0:T(8,128)(2,1)}, f32[256,512]{1,0:T(8,128)}, f32[2,256]{1,0:T(2,128)}, f32[256,47]{1,0:T(8,128)}, /*index=5*/f32[1,47]{1,0:T(1,128)}, f32[1,47]{1,0:T(1,128)}) custom-call(f32[1]{0:T(128)} %bitcast.3.lc_ref, f8e4m3fn[4096,4096]{1,0:T(32,128)(4,1)} %get-tuple-element.53.a_ref, ...), custom_call_target="tpu_custom_call" | custom-call | flops 15032385536 | bytes 33554432 | tf_op jit(solution)/shard_map/top_step/pallas_call | solution.py:376
  331.1 13.3 %spread_far.2 = bf16[4096,256]{1,0:T(8,128)(2,1)} custom-call(f8e4m3fn[4096,4096]{1,0:T(32,128)(4,1)} %get-tuple-element.53.a_ref, bf16[4096,256]{1,0:T(8,128)(2,1)} %get-tuple-element.61.d_ref), custom_call_target="tpu_custom_call" | custom-call | flops 8589934592 | bytes 16777216 | tf_op jit(solution)/shard_map/spread_far/pallas_call | solution.py:483
  350.6 12.2 %collective-permute-done.26 = bf16[1024,256]{1,0:T(8,128)(2,1)S(1)} collective-permute-done((bf16[1024,256]{1,0:T(8,128)(2,1)S(1)}, bf16[1024,256]{1,0:T(8,128)(2,1)S(1)}, u32[]{:S(2)}, u32[]{:S(2)}) %collective-permute-start.26) | collective-permute-done | bytes 524320 | tf_op jit(solution)/shard_map/ppermute | solution.py:48
  364.0 14.3 %spread_near.2.dh_ref = f32[4096,256]{1,0:T(8,128)} custom-call(f8e4m3fn[4096,4096]{1,0:T(32,128)(4,1)} %get-tuple-element.52.a_ref, bf16[4096,256]{1,0:T(8,128)(2,1)} %get-tuple-element.61.d_ref, f32[4096,256]{1,0:T(8,128)} %get-tuple-element.62.refs_0_), custom_call_target="tpu_custom_call" | custom-call | flops 8589934592 | bytes 16777216 | tf_op jit(solution)/shard_map/spread_near/pallas_call | solution.py:483
  392.6 14.7 %lower_step.2 = (f32[256,512]{1,0:T(8,128)}, f32[2,256]{1,0:T(2,128)}, f32[4096,256]{1,0:T(8,128)}, bf16[4096,256]{1,0:T(8,128)(2,1)}) custom-call(f32[4096,256]{1,0:T(8,128)} %spread_near.2.dh_ref, f32[128,256]{1,0:T(8,128)} %fusion.3.dshared_ref, s32[3,128]{1,0:T(4,128)} %brow_ref.7, f32[4096,256]{1,0:T(8,128)} %get-tuple-element.63.pre_ref, ...), custom_call_target="tpu_custom_call" | custom-call | flops 4294967296 | bytes 25165824 | tf_op jit(solution)/shard_map/lower_step/pallas_call | solution.py:446
  407.4 13.3 %spread_far.3 = bf16[4096,256]{1,0:T(8,128)(2,1)} custom-call(f8e4m3fn[4096,4096]{1,0:T(32,128)(4,1)} %get-tuple-element.54.a_ref, bf16[4096,256]{1,0:T(8,128)(2,1)} %get-tuple-element.65.d_ref), custom_call_target="tpu_custom_call" | custom-call | flops 8589934592 | bytes 16777216 | tf_op jit(solution)/shard_map/spread_far/pallas_call | solution.py:483
  424.0 4.2 collective-permute-done.46
  441.4 5.3 collective-permute-done.31
  447.8 14.3 %spread_near.3.dh_ref = f32[4096,256]{1,0:T(8,128)} custom-call(f8e4m3fn[4096,4096]{1,0:T(32,128)(4,1)} %get-tuple-element.51.a_ref, bf16[4096,256]{1,0:T(8,128)(2,1)} %get-tuple-element.65.d_ref, f32[4096,256]{1,0:T(8,128)} %get-tuple-element.66.refs_0_), custom_call_target="tpu_custom_call" | custom-call | flops 8589934592 | bytes 16777216 | tf_op jit(solution)/shard_map/spread_near/pallas_call | solution.py:483
  463.0 4.4 collective-permute-done.33
  473.4 12.7 %lower_step.3 = (f32[256,256]{1,0:T(8,128)}, f32[2,256]{1,0:T(2,128)}) custom-call(f32[4096,256]{1,0:T(8,128)} %spread_near.3.dh_ref, f32[128,256]{1,0:T(8,128)} %fusion.2.dshared_ref, s32[3,128]{1,0:T(4,128)} %brow_ref.7, f32[4096,256]{1,0:T(8,128)} %get-tuple-element.67.pre_ref, bf16[4096,100]{1,0:T(8,128)(2,1)} %copy-done.2, ...), custom_call_target="tpu_custom_call" | custom-call | flops 4294967296 | bytes 25165824 | tf_op jit(solution)/shard_map/lower_step/pallas_call | solution.py:446
  (324 shorter events, 171.1 us)
Async XLA Ops:
  2.9 47.8 %collective-permute-start.10 = (bf16[8,1271]{1,0:T(8,128)(2,1)S(1)}, bf16[8,1271]{1,0:T(8,128)(2,1)S(1)}, u32[]{:S(2)}, u32[]{:S(2)}) collective-permute-start(bf16[8,1271]{1,0:T(8,128)(2,1)S(1)} %concatenate.90), channel_id=1, source_target_pairs={{0,16},{1,17},{2,18},{3,19},{4,20},{5,21},{6,22},{7,23},{8,24},{9,... | collective-permute-start | bytes 61016 | tf_op jit(solution)/shard_map/ppermute | solution.py:48
  8.8 42.5 %collective-permute-start.5 = (bf16[128,100]{1,0:T(8,128)(2,1)S(1)}, bf16[128,100]{1,0:T(8,128)(2,1)S(1)}, u32[]{:S(2)}, u32[]{:S(2)}) collective-permute-start(bf16[128,100]{1,0:T(8,128)(2,1)S(1)} %gather_fusion), channel_id=1, source_target_pairs={{0,16},{1,17},{2,18},{3,19},{4,20},{5,21},{6,22},{7,23},{8,24},{9,... | collective-permute-start | bytes 76808 | tf_op jit(solution)/shard_map/ppermute | solution.py:48
  59.3 6.0 %collective-permute-start.13 = (bf16[64,1271]{1,0:T(8,128)(2,1)S(1)}, bf16[64,1271]{1,0:T(8,128)(2,1)S(1)}, u32[]{:S(2)}, u32[]{:S(2)}) collective-permute-start(bf16[64,1271]{1,0:T(8,128)(2,1)S(1)} %pad_maximum_fusion.5), channel_id=1, source_target_pairs={{0,2},{1,3},{2,0},{3,1},{4,6},{5,7},{6,4},{7,5},{8,10},{9,11},{10,... | collective-permute-start | bytes 488072 | tf_op jit(solution)/shard_map/ppermute | solution.py:48
  61.0 7.1 %collective-permute-start.8 = (bf16[1024,100]{1,0:T(8,128)(2,1)S(1)}, bf16[1024,100]{1,0:T(8,128)(2,1)S(1)}, u32[]{:S(2)}, u32[]{:S(2)}) collective-permute-start(bf16[1024,100]{1,0:T(8,128)(2,1)S(1)} %pad_maximum_fusion.2), channel_id=1, source_target_pairs={{0,2},{1,3},{2,0},{3,1},{4,6},{5,7},{6,4},{7,5},{8,10},{9,11},{10,... | collective-permute-start | bytes 614408 | tf_op jit(solution)/shard_map/ppermute | solution.py:48
  98.3 6.4 %collective-permute-start.16 = (bf16[256,256]{1,0:T(8,128)(2,1)S(1)}, bf16[256,256]{1,0:T(8,128)(2,1)S(1)}, u32[]{:S(2)}, u32[]{:S(2)}) collective-permute-start(bf16[256,256]{1,0:T(8,128)(2,1)S(1)} %pad_maximum_fusion.7), channel_id=1, source_target_pairs={{0,8},{1,9},{2,10},{3,11},{4,12},{5,13},{6,14},{7,15},{8,0},{9,1},... | collective-permute-start | bytes 393224 | tf_op jit(solution)/shard_map/ppermute | solution.py:48
  105.5 7.6 %collective-permute-start.17 = (bf16[512,256]{1,0:T(8,128)(2,1)S(1)}, bf16[512,256]{1,0:T(8,128)(2,1)S(1)}, u32[]{:S(2)}, u32[]{:S(2)}) collective-permute-start(bf16[512,256]{1,0:T(8,128)(2,1)S(1)} %pad_maximum_fusion.3), channel_id=1, source_target_pairs={{0,4},{1,5},{2,6},{3,7},{4,0},{5,1},{6,2},{7,3},{8,12},{9,13},{10,... | collective-permute-start | bytes 786440 | tf_op jit(solution)/shard_map/ppermute | solution.py:48
  113.9 12.2 %collective-permute-start.18 = (bf16[1024,256]{1,0:T(8,128)(2,1)S(1)}, bf16[1024,256]{1,0:T(8,128)(2,1)S(1)}, u32[]{:S(2)}, u32[]{:S(2)}) collective-permute-start(bf16[1024,256]{1,0:T(8,128)(2,1)S(1)} %pad_maximum_fusion), channel_id=1, source_target_pairs={{0,2},{1,3},{2,0},{3,1},{4,6},{5,7},{6,4},{7,5},{8,10},{9,11},{10,... | collective-permute-start | bytes 1572872 | tf_op jit(solution)/shard_map/ppermute | solution.py:48
  126.3 42.7 %collective-permute-start.19 = (bf16[2048,256]{1,0:T(8,128)(2,1)S(1)}, bf16[2048,256]{1,0:T(8,128)(2,1)S(1)}, u32[]{:S(2)}, u32[]{:S(2)}) collective-permute-start(bf16[2048,256]{1,0:T(8,128)(2,1)S(1)} %get-tuple-element.111), channel_id=1, source_target_pairs={{0,1},{1,0},{2,3},{3,2},{4,5},{5,4},{6,7},{7,6},{8,9},{9,8},{10,11... | collective-permute-start | bytes 3145736 | tf_op jit(solution)/shard_map/ppermute | solution.py:48
  205.7 7.4 %collective-permute-start.22 = (bf16[512,256]{1,0:T(8,128)(2,1)S(1)}, bf16[512,256]{1,0:T(8,128)(2,1)S(1)}, u32[]{:S(2)}, u32[]{:S(2)}) collective-permute-start(bf16[512,256]{1,0:T(8,128)(2,1)S(1)} %pad_maximum_fusion.4), channel_id=1, source_target_pairs={{0,4},{1,5},{2,6},{3,7},{4,0},{5,1},{6,2},{7,3},{8,12},{9,13},{10,... | collective-permute-start | bytes 786440 | tf_op jit(solution)/shard_map/ppermute | solution.py:48
  214.0 12.1 %collective-permute-start.23 = (bf16[1024,256]{1,0:T(8,128)(2,1)S(1)}, bf16[1024,256]{1,0:T(8,128)(2,1)S(1)}, u32[]{:S(2)}, u32[]{:S(2)}) collective-permute-start(bf16[1024,256]{1,0:T(8,128)(2,1)S(1)} %pad_maximum_fusion.1), channel_id=1, source_target_pairs={{0,2},{1,3},{2,0},{3,1},{4,6},{5,7},{6,4},{7,5},{8,10},{9,11},{10,... | collective-permute-start | bytes 1572872 | tf_op jit(solution)/shard_map/ppermute | solution.py:48
  216.4 37.6 %collective-permute-start = (f32[1,1]{1,0:T(1,128)}, f32[1,1]{1,0:T(1,128)}, u32[]{:S(2)}, u32[]{:S(2)}) collective-permute-start(f32[1,1]{1,0:T(1,128)} %bitcast.2), channel_id=1, source_target_pairs={{0,1},{1,0},{2,3},{3,2},{4,5},{5,4},{6,7},{7,6},{8,9},{9,8},{10,11... | collective-permute-start | bytes 20 | tf_op jit(solution)/shard_map/ppermute | solution.py:48
  226.3 62.7 %collective-permute-start.24 = (bf16[2048,256]{1,0:T(8,128)(2,1)S(1)}, bf16[2048,256]{1,0:T(8,128)(2,1)S(1)}, u32[]{:S(2)}, u32[]{:S(2)}) collective-permute-start(bf16[2048,256]{1,0:T(8,128)(2,1)S(1)} %get-tuple-element.109), channel_id=1, source_target_pairs={{0,1},{1,0},{2,3},{3,2},{4,5},{5,4},{6,7},{7,6},{8,9},{9,8},{10,11... | collective-permute-start | bytes 3145736 | tf_op jit(solution)/shard_map/ppermute | solution.py:48
  348.8 14.0 %collective-permute-start.26 = (bf16[1024,256]{1,0:T(8,128)(2,1)S(1)}, bf16[1024,256]{1,0:T(8,128)(2,1)S(1)}, u32[]{:S(2)}, u32[]{:S(2)}) collective-permute-start(bf16[1024,256]{1,0:T(8,128)(2,1)S(1)} %slice.335), channel_id=1, source_target_pairs={{0,2},{1,3},{2,0},{3,1},{4,6},{5,7},{6,4},{7,5},{8,10},{9,11},{10,... | collective-permute-start | bytes 1572872 | tf_op jit(solution)/shard_map/ppermute | solution.py:48
  350.5 28.6 %collective-permute-start.50 = (f32[128,47]{1,0:T(8,128)S(1)}, f32[128,47]{1,0:T(8,128)S(1)}, u32[]{:S(2)}, u32[]{:S(2)}) collective-permute-start(f32[128,47]{1,0:T(8,128)S(1)} %slice.305), channel_id=1, source_target_pairs={{0,1},{1,0},{2,3},{3,2},{4,5},{5,4},{6,7},{7,6},{8,9},{9,8},{10,11... | collective-permute-start | bytes 72200 | tf_op jit(solution)/shard_map/ppermute | solution.py:48
  362.9 18.0 %collective-permute-start.27 = (bf16[512,256]{1,0:T(8,128)(2,1)S(1)}, bf16[512,256]{1,0:T(8,128)(2,1)S(1)}, u32[]{:S(2)}, u32[]{:S(2)}) collective-permute-start(bf16[512,256]{1,0:T(8,128)(2,1)S(1)} %slice.337), channel_id=1, source_target_pairs={{0,4},{1,5},{2,6},{3,7},{4,0},{5,1},{6,2},{7,3},{8,12},{9,13},{10,... | collective-permute-start | bytes 786440 | tf_op jit(solution)/shard_map/ppermute | solution.py:48
  378.4 43.8 %collective-permute-start.45 = (f32[128,512]{1,0:T(8,128)S(1)}, f32[128,512]{1,0:T(8,128)S(1)}, u32[]{:S(2)}, u32[]{:S(2)}) collective-permute-start(f32[128,512]{1,0:T(8,128)S(1)} %slice.295), channel_id=1, source_target_pairs={{0,1},{1,0},{2,3},{3,2},{4,5},{5,4},{6,7},{7,6},{8,9},{9,8},{10,11... | collective-permute-start | bytes 786440 | tf_op jit(solution)/shard_map/ppermute | solution.py:48
  387.3 35.4 %collective-permute-start.53 = (f32[16,47]{1,0:T(8,128)S(1)}, f32[16,47]{1,0:T(8,128)S(1)}, u32[]{:S(2)}, u32[]{:S(2)}) collective-permute-start(f32[16,47]{1,0:T(8,128)S(1)} %slice.383), channel_id=1, source_target_pairs={{0,8},{1,9},{2,10},{3,11},{4,12},{5,13},{6,14},{7,15},{8,0},{9,1},... | collective-permute-start | bytes 9032 | tf_op jit(solution)/shard_map/ppermute | solution.py:48
  422.1 12.3 %collective-permute-start.30 = (bf16[2048,256]{1,0:T(8,128)(2,1)S(1)}, bf16[2048,256]{1,0:T(8,128)(2,1)S(1)}, u32[]{:S(2)}, u32[]{:S(2)}) collective-permute-start(bf16[2048,256]{1,0:T(8,128)(2,1)S(1)} %slice.343), channel_id=1, source_target_pairs={{0,1},{1,0},{2,3},{3,2},{4,5},{5,4},{6,7},{7,6},{8,9},{9,8},{10,11... | collective-permute-start | bytes 3145736 | tf_op jit(solution)/shard_map/ppermute | solution.py:48
  422.3 6.0 %collective-permute-start.46 = (f32[64,512]{1,0:T(8,128)S(1)}, f32[64,512]{1,0:T(8,128)S(1)}, u32[]{:S(2)}, u32[]{:S(2)}) collective-permute-start(f32[64,512]{1,0:T(8,128)S(1)} %slice.371), channel_id=1, source_target_pairs={{0,2},{1,3},{2,0},{3,1},{4,6},{5,7},{6,4},{7,5},{8,10},{9,11},{10,... | collective-permute-start | bytes 393224 | tf_op jit(solution)/shard_map/ppermute | solution.py:48
  422.7 6.5 %collective-permute-start.54 = (f32[8,47]{1,0:T(8,128)S(1)}, f32[8,47]{1,0:T(8,128)S(1)}, u32[]{:S(2)}, u32[]{:S(2)}) collective-permute-start(f32[8,47]{1,0:T(8,128)S(1)} %slice.385), channel_id=1, source_target_pairs={{0,16},{1,17},{2,18},{3,19},{4,20},{5,21},{6,22},{7,23},{8,24},{9,... | collective-permute-start | bytes 4520 | tf_op jit(solution)/shard_map/ppermute | solution.py:48
  434.6 12.2 %collective-permute-start.31 = (bf16[1024,256]{1,0:T(8,128)(2,1)S(1)}, bf16[1024,256]{1,0:T(8,128)(2,1)S(1)}, u32[]{:S(2)}, u32[]{:S(2)}) collective-permute-start(bf16[1024,256]{1,0:T(8,128)(2,1)S(1)} %slice.345), channel_id=1, source_target_pairs={{0,2},{1,3},{2,0},{3,1},{4,6},{5,7},{6,4},{7,5},{8,10},{9,11},{10,... | collective-permute-start | bytes 1572872 | tf_op jit(solution)/shard_map/ppermute | solution.py:48
  441.4 21.1 %collective-permute-start.40 = (f32[128,512]{1,0:T(8,128)S(1)}, f32[128,512]{1,0:T(8,128)S(1)}, u32[]{:S(2)}, u32[]{:S(2)}) collective-permute-start(f32[128,512]{1,0:T(8,128)S(1)} %slice.285), channel_id=1, source_target_pairs={{0,1},{1,0},{2,3},{3,2},{4,5},{5,4},{6,7},{7,6},{8,9},{9,8},{10,11... | collective-permute-start | bytes 786440 | tf_op jit(solution)/shard_map/ppermute | solution.py:48
  446.8 15.2 %collective-permute-start.32 = (bf16[512,256]{1,0:T(8,128)(2,1)S(1)}, bf16[512,256]{1,0:T(8,128)(2,1)S(1)}, u32[]{:S(2)}, u32[]{:S(2)}) collective-permute-start(bf16[512,256]{1,0:T(8,128)(2,1)S(1)} %slice.347), channel_id=1, source_target_pairs={{0,4},{1,5},{2,6},{3,7},{4,0},{5,1},{6,2},{7,3},{8,12},{9,13},{10,... | collective-permute-start | bytes 786440 | tf_op jit(solution)/shard_map/ppermute | solution.py:48
  467.6 19.7 %collective-permute-start.42 = (f32[32,512]{1,0:T(8,128)S(1)}, f32[32,512]{1,0:T(8,128)S(1)}, u32[]{:S(2)}, u32[]{:S(2)}) collective-permute-start(f32[32,512]{1,0:T(8,128)S(1)} %slice.365), channel_id=1, source_target_pairs={{0,4},{1,5},{2,6},{3,7},{4,0},{5,1},{6,2},{7,3},{8,12},{9,13},{10,... | collective-permute-start | bytes 196616 | tf_op jit(solution)/shard_map/ppermute | solution.py:48
  (72 other events, 1150.1 us)
